TPU v7x, 32 devices: a whole 2x2x4 slice. The times are simulated.
32 devices in a mesh: ctx: 8 (over z, y), head: 4 (over x, core).
Axes of the slice: x: 2, y: 2, z: 4, core: 2. Of those that a mesh axis runs over, the one named last changes fastest.
Arguments:
- queries: bfloat16 [8192, 4096], P('ctx', 'head'), may hold values from -6 to 6
- keys: bfloat16 [8192, 1024], P('ctx', 'head'), may hold values from -6 to 6
- values: bfloat16 [8192, 1024], P('ctx', 'head'), may hold values from -6 to 6
- block_masks: int32 [32, 64], P('head', 'ctx'), may hold values from 0 to 63
- residual: bfloat16 [8192, 4096], P(('ctx', 'head')), may hold values from -1.5 to 1.5
- norm_gain: bfloat16 [4096], replicated, may hold values from 0.099609375 to 1.8984375
Outputs:
- stream: bfloat16 [8192, 4096], P(('ctx', 'head'))
- normed: bfloat16 [8192, 4096], P(('ctx', 'head'))
Inputs may be any that keep to these rules, and one draw needn't show every extreme that they name: Bit b of block_masks[h, i] says whether query block i of head h attends to block i XOR 2^b; it is read only where that block comes earlier, and bits from 6 up are zero.
All inputs are finite; a program needn't handle non-finite values.
Results may differ from a plain program's by a relative error of at most 0.0052.
Values may be sent and summed in bfloat16 or wider, within the bound.
A program may use at most 64 MiB of HBM per device.

v0:
```python
import jax
import jax.numpy as jnp
from jax import lax
from jax.sharding import PartitionSpec as P

DH = 128
BLOCK = 128


MASKED_SCORE = -1e30
EPSILON = 1e-05


def passed_along(block, axis, distance):
    devices = range(lax.axis_size(axis))
    route = [(i - distance, i) for i in devices if i - distance in devices]
    return lax.ppermute(block, axis, route)


def split_upper(source, axis_at, stride):
    extent = source.shape
    length = extent[axis_at]
    folded = source.reshape(
        extent[:axis_at] + (length // (2 * stride), 2, stride) + extent[axis_at + 1 :]
    )
    low_part = lax.index_in_dim(folded, 0, axis_at + 1, keepdims=False)
    high_part = lax.index_in_dim(folded, 1, axis_at + 1, keepdims=False)
    flattened = extent[:axis_at] + (length // 2,) + extent[axis_at + 1 :]
    return (low_part.reshape(flattened), high_part.reshape(flattened))


def join_halves(low_part, high_part, axis_at, stride):
    extent = low_part.shape
    length = extent[axis_at]
    folded = extent[:axis_at] + (length // stride, 1, stride) + extent[axis_at + 1 :]
    stacked = jnp.concatenate(
        [low_part.reshape(folded), high_part.reshape(folded)], axis=axis_at + 1
    )
    return stacked.reshape(extent[:axis_at] + (length * 2,) + extent[axis_at + 1 :])


def to_blocks(source, head_count):
    length = source.shape[0]
    return source.reshape(length // BLOCK, BLOCK, head_count, DH).transpose(2, 0, 1, 3)


def level_flags(bitmap, bit_level):
    return jnp.right_shift(bitmap, bit_level) & 1 == 1


def fresh_state(groups, head_count, blocks):
    return (
        jnp.full((groups, head_count, blocks, BLOCK), MASKED_SCORE, jnp.float32),
        jnp.zeros((groups, head_count, blocks, BLOCK), jnp.float32),
        jnp.zeros((groups, head_count, blocks, BLOCK, DH), jnp.float32),
    )


def update(running, query_part, key_part, value_part, allowed):
    row_max, row_sum, weighted = running
    scores = jnp.einsum(
        "gjnqd,gnkd->gjnqk", query_part, key_part, preferred_element_type=jnp.float32
    ) * DH ** (-0.5)
    scores = jnp.where(allowed, scores, MASKED_SCORE)
    new_max = jnp.maximum(row_max, scores.max(-1))
    factor = jnp.exp(row_max - new_max)
    weights = jnp.where(allowed, jnp.exp(scores - new_max[..., None]), 0.0)
    new_sum = row_sum * factor + weights.sum(-1)
    new_weighted = weighted * factor[..., None] + jnp.einsum(
        "gjnqk,gnkd->gjnqd",
        weights.astype(jnp.bfloat16),
        value_part,
        preferred_element_type=jnp.float32,
    )
    return (new_max, new_sum, new_weighted)


def fetch_partner(keys, values, bit_level):
    return passed_along((keys, values), "ctx", 2**bit_level)


def shards(queries, keys, values, block_masks, residual, norm_gain):
    tokens = queries.shape[0]
    blocks = tokens // BLOCK
    groups = keys.shape[1] // DH
    per_group = queries.shape[1] // keys.shape[1]
    query_blocks = queries.reshape(blocks, BLOCK, groups, per_group, DH).transpose(2, 3, 0, 1, 4)
    key_blocks = to_blocks(keys, groups)
    value_blocks = to_blocks(values, groups)
    head_bits = block_masks.reshape(groups, per_group, blocks)
    local_bits = blocks.bit_length() - 1
    ctx_bits = lax.axis_size("ctx").bit_length() - 1
    ctx_index = lax.axis_index("ctx")
    causal = lax.broadcasted_iota(jnp.int32, (BLOCK, BLOCK), 0) >= lax.broadcasted_iota(
        jnp.int32, (BLOCK, BLOCK), 1
    )
    running = update(
        fresh_state(groups, per_group, blocks), query_blocks, key_blocks, value_blocks, causal
    )
    for bit_level in range(local_bits):
        stride = 2**bit_level
        _, query_high = split_upper(query_blocks, 2, stride)
        key_low, _ = split_upper(key_blocks, 1, stride)
        value_low, _ = split_upper(value_blocks, 1, stride)
        _, bits_high = split_upper(head_bits, 2, stride)
        allowed = level_flags(bits_high, bit_level)[..., None, None]
        divided = [split_upper(portion, 2, stride) for portion in running]
        upper_state = update(
            tuple((halves_pair[1] for halves_pair in divided)),
            query_high,
            key_low,
            value_low,
            allowed,
        )
        running = tuple(
            (
                join_halves(halves_pair[0], portion, 2, stride)
                for halves_pair, portion in zip(divided, upper_state)
            )
        )
    sequence_bits = list(range(ctx_bits))
    for bit_level in sequence_bits:
        far_keys, far_values = fetch_partner(keys, values, bit_level)
        bit_set = jnp.right_shift(ctx_index, bit_level) & 1 == 1
        far_key_blocks = to_blocks(far_keys, groups)
        far_value_blocks = to_blocks(far_values, groups)
        remote_allowed = level_flags(head_bits, local_bits + bit_level)[..., None, None]
        running = lax.cond(
            bit_set,
            lambda state: update(
                state, query_blocks, far_key_blocks, far_value_blocks, remote_allowed
            ),
            lambda state: state,
            running,
        )
    row_max, row_sum, weighted = running
    attended = (weighted / row_sum[..., None]).astype(jnp.bfloat16)
    attended = attended.transpose(2, 3, 0, 1, 4).reshape(tokens, groups * per_group * DH)
    gathered = lax.all_to_all(attended, "head", split_axis=0, concat_axis=1, tiled=True)
    summed = residual.astype(jnp.float32) + gathered.astype(jnp.float32)
    stream = summed.astype(jnp.bfloat16)
    normed = (
        summed
        * lax.rsqrt(jnp.mean(summed * summed, axis=-1, keepdims=True) + EPSILON)
        * norm_gain.astype(jnp.float32)
    )
    return (stream, normed.astype(jnp.bfloat16))


def solution(mesh):
    in_specs = (
        P("ctx", "head"),
        P("ctx", "head"),
        P("ctx", "head"),
        P("head", "ctx"),
        P(("ctx", "head"), None),
        P(),
    )
    out_specs = (P(("ctx", "head"), None), P(("ctx", "head"), None))
    return jax.shard_map(shards, mesh=mesh, in_specs=in_specs, out_specs=out_specs, check_vma=False)
```

profile of v0, /device:TPU:28, one launch (start us, length us, event | category | flops | bytes accessed | tf_op | source)
XLA Modules:
  0.0 198.0 jit_solution(157070211265948676)
XLA Ops:
  9.5 3.2 %reshape.305 = bf16[8,128,2,4,128]{4,3,2,1,0:T(4,128)(2,1)S(1)} reshape(bf16[1024,1024]{1,0:T(8,128)(2,1)} %param.12) | data formatting | bytes 4194304 | tf_op jit(solution)/shard_map/reshape | solution.py:87
  15.9 2.8 %copy.502 = bf16[8,128,2,4,128]{1,0,4,3,2:T(8,128)(2,1)S(1)} copy(bf16[8,128,2,4,128]{4,3,2,1,0:T(4,128)(2,1)} %copy-done.2) | data formatting | bytes 4194304 | tf_op jit(solution)/shard_map/reshape | solution.py:87
  27.9 4.4 %bitcast_add_fusion.4 = f32[2,4,8,128,128]{4,3,1,2,0:T(8,128)S(1)} fusion(f32[2,8,128,4,128]{4,2,3,1,0:T(8,128)} %copy-done.5, f32[2,4,8,128]{3,1,2,0:T(4,128)S(1)} %get-tuple-element.299, f32[2,4,8,128]{3,1,2,0:T(4,128)S(1)} %get-tuple-element.300, pred[128,128]{0,1:T(8,128)(4,1)S(1)} %iota_compare_fusion, bf16[8,128,2,128]{3,2,1,0:T(2,128)(2,1)S(1)} %reshape.306), kind=kOutput, calls=%fused_computation.72 | convolution fusion | flops 274726912 | bytes 8994816 | tf_op jit(solution)/shard_map/gjnqk,gnkd->gjnqd/dot_general | solution.py:69
  42.1 2.5 %copy.526 = bf16[2,4,2,1,2,128,128]{6,5,1,4,2,0,3:T(8,128)(2,1)S(1)} copy(bf16[2,4,2,1,2,128,128]{5,4,3,2,6,1,0:T(2,128)(2,1)} %slice.129) | data formatting | bytes 2097152
  52.3 3.0 %bitcast_add_fusion.5 = f32[2,4,4,128,128]{4,3,1,2,0:T(8,128)S(1)} fusion(f32[2,4,4,128,128]{4,3,1,2,0:T(8,128)} %bitcast.323, bf16[2,4,128,128,1]{3,2,4,1,0:T(8,128)(2,1)S(1)} %bitcast.348, f32[2,4,128,4,128]{4,2,3,1,0:T(8,128)S(1)} %copy-done.3, f32[2,4,4,128]{3,1,2,0:T(4,128)S(1)} %get-tuple-element.297, f32[2,4,4,128]{3,1,2,0:T(4,128)S(1)} %get-tuple-element.298, ...), kind=kOutput, calls=%fused_computation.91 | convolution fusion | flops 137887744 | bytes 6586400 | tf_op jit(solution)/shard_map/gjnqk,gnkd->gjnqd/dot_general | solution.py:69
  79.7 17.3 %collective-permute-done.5 = bf16[1024,256]{1,0:T(8,128)(2,1)} collective-permute-done((bf16[1024,256]{1,0:T(8,128)(2,1)}, bf16[1024,256]{1,0:T(8,128)(2,1)}, u32[]{:S(2)}, u32[]{:S(2)}) %collective-permute-start.5) | collective-permute-done | bytes 524320 | tf_op jit(solution)/shard_map/ppermute | solution.py:17
  100.4 11.3 %conditional.3 = (f32[2,4,8,128]{3,1,2,0:T(4,128)}, f32[2,4,8,128]{3,1,2,0:T(4,128)S(1)}, f32[2,4,8,128,128]{4,3,1,2,0:T(8,128)}) conditional(s32[]{:T(128)} %convert_element_type.59, (f32[2,4,8,128]{3,2,1,0:T(8,128)S(1)}, f32[2,4,8,128]{3,2,1,0:T(8,128)S(1)}, f32[2,4,8,128,128]{4,3,2,1,0:T(8,128)}) %tuple.119, ...), branch_computations={%region_8.9_spmd, %region_9.12_spmd} | conditional | flops 552615936 | bytes 43450768 | solution.py:128
  106.7 5.0 %bitcast_add_fusion = f32[2,4,8,128,128]{4,3,1,2,0:T(8,128)} fusion(f32[2,4,8,128,128]{4,3,2,1,0:T(8,128)S(1)} %copy-done, f32[2,8,128,4,128]{4,2,3,1,0:T(8,128)S(1)} %get-tuple-element.286, f32[2,4,8,128]{3,1,2,0:T(4,128)S(1)} %get-tuple-element.274, f32[2,4,8,128]{3,1,2,0:T(4,128)} %copy_maximum_fusion, pred[2,4,8]{1,2,0:T(8,128)(4,1)S(1)} %copy.378, ...), kind=kOutput, calls=%fused_computation | convolution fusion | flops 275775488 | bytes 13172800 | tf_op jit(solution)/shard_map/cond/branch_1_fun/gjnqk,gnkd->gjnqd/dot_general | solution.py:69
  111.7 12.4 %conditional.4 = ((f32[2,4,8,128]{3,1,2,0:T(4,128)}, f32[2,4,8,128]{3,1,2,0:T(4,128)S(1)}, f32[2,4,8,128,128]{4,3,1,2,0:T(8,128)})) conditional(s32[]{:T(128)} %convert_element_type.58, (f32[2,4,8,128]{3,1,2,0:T(4,128)}, f32[2,4,8,128]{3,1,2,0:T(4,128)S(1)}, f32[2,4,8,128,128]{4,3,1,2,0:T(8,128)}) %conditional.3, ...), branch_computations={%region_12.13_spmd, %region_13.16_spmd} | conditional | flops 552616128 | bytes 26739388 | solution.py:128
  117.4 6.2 %bitcast_add_fusion.1 = f32[2,4,8,128,128]{4,3,1,2,0:T(8,128)} fusion(f32[2,4,8,128,128]{4,3,1,2,0:T(8,128)} %get-tuple-element.118, f32[2,8,128,4,128]{4,2,3,1,0:T(8,128)S(1)} %get-tuple-element.288, f32[2,4,8,128]{3,1,2,0:T(4,128)S(1)} %bitcast.366, f32[2,4,8,128]{3,1,2,0:T(4,128)S(1)} %max.45, pred[2,4,8]{1,2,0:T(8,128)(4,1)S(1)} %copy.380, ...), kind=kOutput, calls=%fused_computation.23 | convolution fusion | flops 275775488 | bytes 13172800 | tf_op jit(solution)/shard_map/cond/branch_1_fun/gjnqk,gnkd->gjnqd/dot_general | solution.py:69
  124.2 10.8 %conditional.5 = ((f32[2,4,8,128]{3,1,2,0:T(4,128)S(1)}, f32[2,4,8,128,128]{4,3,1,2,0:T(8,128)})) conditional(s32[]{:T(128)} %convert_element_type.57, (f32[2,4,8,128]{3,1,2,0:T(4,128)S(1)}, f32[2,4,8,128,128]{4,3,1,2,0:T(8,128)}) %tuple.39, (s32[2,4,8,1,1]{2,1,0,4,3:T(4,128)S(1)}, bf16[2,8,128,128]{2,1,3,0:T(8,128)(2,1)S(1)}, ...), branch_computations={%region_16.17_spmd, %region_17.20_spmd} | conditional | flops 552616128 | bytes 24576664 | solution.py:128
  128.8 6.2 %bitcast_add_fusion.2 = f32[2,4,8,128,128]{4,3,1,2,0:T(8,128)} fusion(f32[2,4,8,128,128]{4,3,1,2,0:T(8,128)} %get-tuple-element.125, f32[2,8,128,4,128]{4,2,3,1,0:T(8,128)S(1)} %get-tuple-element.290, f32[2,4,8,128]{3,1,2,0:T(4,128)S(1)} %bitcast.365, f32[2,4,8,128]{3,1,2,0:T(4,128)S(1)} %max.46, pred[2,4,8]{1,2,0:T(8,128)(4,1)S(1)} %copy.382, ...), kind=kOutput, calls=%fused_computation.45 | convolution fusion | flops 275775488 | bytes 13172800 | tf_op jit(solution)/shard_map/cond/branch_1_fun/gjnqk,gnkd->gjnqd/dot_general | solution.py:69
  135.0 2.9 %fusion.68 = bf16[8,128,2,4,128]{4,1,3,0,2:T(8,128)(2,1)S(1)} fusion(f32[2,4,8,128,128]{4,3,1,2,0:T(8,128)} %get-tuple-element.143, f32[2,4,8,128]{3,1,2,0:T(4,128)S(1)} %get-tuple-element.144), kind=kLoop, calls=%fused_computation.105 | loop fusion | flops 2097152 | bytes 6324224 | tf_op jit(solution)/shard_map/transpose | solution.py:138
  137.8 2.9 %copy.463 = bf16[8,128,2,4,128]{4,3,2,1,0:T(4,128)(2,1)} copy(bf16[8,128,2,4,128]{4,1,3,0,2:T(8,128)(2,1)S(1)} %fusion.68) | data formatting | bytes 4194304 | tf_op jit(solution)/shard_map/transpose | solution.py:138
  140.8 4.4 %all_to_all.10 = bf16[4,256,1024]{2,1,0:T(8,128)(2,1)} reshape(bf16[8,128,2,4,128]{4,3,2,1,0:T(4,128)(2,1)} %copy.463) | data formatting | bytes 4194304 | tf_op jit(solution)/shard_map/all_to_all | solution.py:139
  145.2 4.5 %all-to-all-start = ((bf16[4,256,1024]{2,1,0:T(8,128)(2,1)}), bf16[4,256,1024]{2,1,0:T(8,128)(2,1)}, u32[]{:S(2)}, u32[]{:S(2)}) async-start(bf16[4,256,1024]{2,1,0:T(8,128)(2,1)} %all_to_all.10), calls=%async_computation | async-start | bytes 4194304 | tf_op jit(solution)/shard_map/all_to_all | solution.py:139
  149.7 3.3 %copy.384 = bf16[256,4096]{0,1:T(8,128)(2,1)S(1)} copy(bf16[256,4096]{1,0:T(8,128)(2,1)} %param.16) | data formatting | bytes 4194304 | tf_op args[4]
  153.0 22.4 %all-to-all-done = bf16[4,256,1024]{2,1,0:T(8,128)(2,1)} async-done(((bf16[4,256,1024]{2,1,0:T(8,128)(2,1)}), bf16[4,256,1024]{2,1,0:T(8,128)(2,1)}, u32[]{:S(2)}, u32[]{:S(2)}) %all-to-all-start) | async-done | bytes 2097184 | tf_op jit(solution)/shard_map/all_to_all | solution.py:139
  175.4 4.0 %convert_bitcast_fusion = f32[256,4,1024]{2,0,1:T(8,128)} fusion(bf16[4,256,1024]{2,1,0:T(8,128)(2,1)} %all-to-all-done), kind=kLoop, calls=%fused_computation.74 | loop fusion | flops 1048576 | bytes 6291456 | tf_op jit(solution)/shard_map/convert_element_type | solution.py:140
  179.4 5.4 %copy.464 = f32[256,4,1024]{0,2,1:T(8,128)} copy(f32[256,4,1024]{2,0,1:T(8,128)} %convert_bitcast_fusion) | data formatting | bytes 8388608 | tf_op jit(solution)/shard_map/convert_element_type | solution.py:140
  184.8 2.9 %multiply_reduce_fusion = f32[256]{0:T(256)S(1)} fusion(f32[256,4,1024]{0,2,1:T(8,128)} %copy.464, bf16[256,4096]{0,1:T(8,128)(2,1)S(1)} %copy.384), kind=kLoop, calls=%fused_computation.76 | loop fusion | flops 4194048 | bytes 6292480 | tf_op jit(solution)/shard_map/reduce_sum | solution.py:144
  188.3 2.7 %multiply_convert_fusion = (bf16[256,4096]{0,1:T(8,128)(2,1)}, bf16[256,4096]{0,1:T(8,128)(2,1)}) fusion(f32[4096]{0:T(1024)S(1)} %convert_element_type.69, f32[256]{0:T(256)S(1)} %add_rsqrt_fusion, f32[256,4,1024]{0,2,1:T(8,128)S(1)} %copy-done.1, bf16[256,4096]{0,1:T(8,128)(2,1)S(1)} %copy.384), kind=kLoop, calls=%fused_computation.75 | loop fusion | flops 6291456 | bytes 10503168 | tf_op jit(solution)/shard_map/convert_element_type | solution.py:147
  191.0 4.2 %copy.465 = bf16[256,4096]{1,0:T(8,128)(2,1)} copy(bf16[256,4096]{0,1:T(8,128)(2,1)} %get-tuple-element.292) | data formatting | bytes 4194304
  195.2 2.8 %copy.466 = bf16[256,4096]{1,0:T(8,128)(2,1)} copy(bf16[256,4096]{0,1:T(8,128)(2,1)S(1)} %copy-done.6) | data formatting | bytes 4194304
  (153 shorter events, 83.5 us)
Async XLA Ops:
  0.6 64.2 %collective-permute-start = (bf16[1024,256]{1,0:T(8,128)(2,1)}, bf16[1024,256]{1,0:T(8,128)(2,1)}, u32[]{:S(2)}, u32[]{:S(2)}) collective-permute-start(bf16[1024,256]{1,0:T(8,128)(2,1)} %param.13), channel_id=1, source_target_pairs={{0,4},{4,8},{8,12},{12,16},{16,20},{20,24},{24,28},{1,5},{5,9},{9,... | collective-permute-start | bytes 1572872 | tf_op jit(solution)/shard_map/ppermute | solution.py:17
  1.9 71.6 %collective-permute-start.2 = (bf16[1024,256]{1,0:T(8,128)(2,1)}, bf16[1024,256]{1,0:T(8,128)(2,1)}, u32[]{:S(2)}, u32[]{:S(2)}) collective-permute-start(bf16[1024,256]{1,0:T(8,128)(2,1)} %param.13), channel_id=1, source_target_pairs={{0,8},{4,12},{8,16},{12,20},{16,24},{20,28},{1,9},{5,13},{9,17},{1... | collective-permute-start | bytes 1572872 | tf_op jit(solution)/shard_map/ppermute | solution.py:17
  3.2 68.0 %collective-permute-start.1 = (bf16[1024,256]{1,0:T(8,128)(2,1)}, bf16[1024,256]{1,0:T(8,128)(2,1)}, u32[]{:S(2)}, u32[]{:S(2)}) collective-permute-start(bf16[1024,256]{1,0:T(8,128)(2,1)} %param.14), channel_id=1, source_target_pairs={{0,4},{4,8},{8,12},{12,16},{16,20},{20,24},{24,28},{1,5},{5,9},{9,... | collective-permute-start | bytes 1572872 | tf_op jit(solution)/shard_map/ppermute | solution.py:17
  4.5 71.3 %collective-permute-start.3 = (bf16[1024,256]{1,0:T(8,128)(2,1)}, bf16[1024,256]{1,0:T(8,128)(2,1)}, u32[]{:S(2)}, u32[]{:S(2)}) collective-permute-start(bf16[1024,256]{1,0:T(8,128)(2,1)} %param.14), channel_id=1, source_target_pairs={{0,8},{4,12},{8,16},{12,20},{16,24},{20,28},{1,9},{5,13},{9,17},{1... | collective-permute-start | bytes 1572872 | tf_op jit(solution)/shard_map/ppermute | solution.py:17
  5.8 72.4 %collective-permute-start.4 = (bf16[1024,256]{1,0:T(8,128)(2,1)}, bf16[1024,256]{1,0:T(8,128)(2,1)}, u32[]{:S(2)}, u32[]{:S(2)}) collective-permute-start(bf16[1024,256]{1,0:T(8,128)(2,1)} %param.13), channel_id=1, source_target_pairs={{0,16},{4,20},{8,24},{12,28},{1,17},{5,21},{9,25},{13,29},{2,18},{... | collective-permute-start | bytes 1572872 | tf_op jit(solution)/shard_map/ppermute | solution.py:17
  15.9 2.8 %copy-start.17 = (s32[8,8]{1,0:T(8,128)S(1)}, s32[8,8]{1,0:T(8,128)}, u32[]{:S(2)}) copy-start(s32[8,8]{1,0:T(8,128)} %param.15) | copy-start | bytes 772
  25.7 1.9 copy-start.5
  32.3 1.6 copy-start.12
  32.3 1.7 copy-start.15
  47.6 1.9 copy-start.14
  49.9 2.4 %copy-start.3 = (f32[2,4,128,4,128]{4,2,3,1,0:T(8,128)S(1)}, f32[2,4,128,4,128]{4,2,3,1,0:T(8,128)}, u32[]{:S(2)}) copy-start(f32[2,4,128,4,128]{4,2,3,1,0:T(8,128)} %get-tuple-element.318) | copy-start | bytes 6291460
  52.3 3.0 %copy-start.7 = (f32[2,4,2,1,2,128,128]{6,5,1,3,2,0,4:T(8,128)S(1)}, f32[2,4,2,1,2,128,128]{6,5,1,3,2,0,4:T(8,128)}, u32[]{:S(2)}) copy-start(f32[2,4,2,1,2,128,128]{6,5,1,3,2,0,4:T(8,128)} %get-tuple-element.293) | copy-start | bytes 6291460
  58.4 2.2 %copy-start.13 = (bf16[8,128,2,4,128]{4,1,0,3,2:T(8,128)(2,1)S(1)}, bf16[8,128,2,4,128]{4,1,0,3,2:T(8,128)(2,1)}, u32[]{:S(2)}) copy-start(bf16[8,128,2,4,128]{4,1,0,3,2:T(8,128)(2,1)} %copy.505) | copy-start | bytes 6291460
  58.4 2.3 %copy-start.16 = (bf16[8,128,2,128]{3,1,0,2:T(8,128)(2,1)S(1)}, bf16[8,128,2,128]{3,1,0,2:T(8,128)(2,1)}, u32[]{:S(2)}) copy-start(bf16[8,128,2,128]{3,1,0,2:T(8,128)(2,1)} %copy.501) | copy-start | bytes 1572868
  60.7 2.2 %copy-start.4 = (f32[2,4,2,2,2,128,128]{6,5,1,4,3,0,2:T(8,128)S(1)}, f32[2,4,2,2,2,128,128]{6,5,1,4,3,0,2:T(8,128)}, u32[]{:S(2)}) copy-start(f32[2,4,2,2,2,128,128]{6,5,1,4,3,0,2:T(8,128)} %copy.437) | copy-start | bytes 12582916
  61.2 1.9 copy-start.9
  64.9 32.1 %collective-permute-start.5 = (bf16[1024,256]{1,0:T(8,128)(2,1)}, bf16[1024,256]{1,0:T(8,128)(2,1)}, u32[]{:S(2)}, u32[]{:S(2)}) collective-permute-start(bf16[1024,256]{1,0:T(8,128)(2,1)} %param.14), channel_id=1, source_target_pairs={{0,16},{4,20},{8,24},{12,28},{1,17},{5,21},{9,25},{13,29},{2,18},{... | collective-permute-start | bytes 1572872 | tf_op jit(solution)/shard_map/ppermute | solution.py:17
  100.6 6.2 %copy-start.11 = (bf16[2,8,128,128]{2,1,3,0:T(8,128)(2,1)S(1)}, bf16[2,8,128,128]{2,1,3,0:T(8,128)(2,1)}, u32[]{:S(2)}) copy-start(bf16[2,8,128,128]{2,1,3,0:T(8,128)(2,1)} %get-tuple-element.256) | copy-start | bytes 1572868 | tf_op jit(solution)/shard_map/cond
  103.5 3.2 %copy-start = (f32[2,4,8,128,128]{4,3,2,1,0:T(8,128)S(1)}, f32[2,4,8,128,128]{4,3,2,1,0:T(8,128)}, u32[]{:S(2)}) copy-start(f32[2,4,8,128,128]{4,3,2,1,0:T(8,128)} %get-tuple-element.255) | copy-start | bytes 12582916 | tf_op jit(solution)/shard_map/cond
  114.9 2.5 %copy-start.10 = (bf16[2,8,128,128]{2,1,3,0:T(8,128)(2,1)S(1)}, bf16[2,8,128,128]{2,1,3,0:T(8,128)(2,1)}, u32[]{:S(2)}) copy-start(bf16[2,8,128,128]{2,1,3,0:T(8,128)(2,1)} %get-tuple-element.263) | copy-start | bytes 1572868 | tf_op jit(solution)/shard_map/cond
  145.2 30.2 %all-to-all-start = ((bf16[4,256,1024]{2,1,0:T(8,128)(2,1)}), bf16[4,256,1024]{2,1,0:T(8,128)(2,1)}, u32[]{:S(2)}, u32[]{:S(2)}) async-start(bf16[4,256,1024]{2,1,0:T(8,128)(2,1)} %all_to_all.10), calls=%async_computation | async-start | bytes 4194304 | tf_op jit(solution)/shard_map/all_to_all | solution.py:139
  149.7 3.3 %copy-start.18 = (bf16[4096]{0:T(1024)(128)(2,1)S(1)}, bf16[4096]{0:T(1024)(128)(2,1)}, u32[]{:S(2)}) copy-start(bf16[4096]{0:T(1024)(128)(2,1)} %param.17) | copy-start | bytes 24580
  184.8 3.4 %copy-start.1 = (f32[256,4,1024]{0,2,1:T(8,128)S(1)}, f32[256,4,1024]{0,2,1:T(8,128)}, u32[]{:S(2)}) copy-start(f32[256,4,1024]{0,2,1:T(8,128)} %copy.464) | copy-start | bytes 12582916
  191.0 4.2 %copy-start.6 = (bf16[256,4096]{0,1:T(8,128)(2,1)S(1)}, bf16[256,4096]{0,1:T(8,128)(2,1)}, u32[]{:S(2)}) copy-start(bf16[256,4096]{0,1:T(8,128)(2,1)} %get-tuple-element.291) | copy-start | bytes 6291460
  (2 other events, 2.6 us)
where the time goes:
time: 200 us; the launch traced here: 198 us
  local copies, waits for them, and re-layouts  74.3 us (37%)
  waiting for transfers between devices  39.7 us (20%)
  matrix products  39.4 us (20%)
  other arithmetic  31 us (16%)
  starting transfers between devices  12.2 us (6%)
    dot_general x7, matrix products, update(): jnp.einsum('gjnqk,gnkd->gjnqd', weights.astype(jnp.bfloat16), value_part,...  28.3 us
    all_to_all x1, waiting for transfers between devices, shards(): lax.all_to_all(attended, 'head', split_axis=0, concat_axis=1, tiled=True)  22.4 us
    unnamed x42, local copies, waits for them, and re-layouts  19.7 us
    reshape x16, local copies, waits for them, and re-layouts, to_blocks(): source.reshape(length // BLOCK, BLOCK, head_count, DH).transpose(2, 0, 1, 3)  18.7 us
    ppermute x6, waiting for transfers between devices, passed_along(): return lax.ppermute(block, axis, route)  17.3 us
    dot_general x7, matrix products, update(): jnp.einsum('gjnqd,gnkd->gjnqk', query_part, key_part, preferred_element_t...  11.1 us
    reduce_sum x7, other arithmetic, update(): new_sum = row_sum * factor + weights.sum(-1)  11 us
    ppermute x6, starting transfers between devices, passed_along(): return lax.ppermute(block, axis, route)  7.75 us
  transfers between devices with their start and end apart: 7, of which 2 were waited for; matrix products, arithmetic and copies ran while one was open for 35% of the time, Pallas kernels for 0%

commit v1 on v0

v1 whole, which is shorter than its diff:
```python
import functools

import jax
import jax.numpy as jnp
from jax import lax
from jax.experimental import pallas as pl
from jax.experimental.pallas import tpu as pltpu
from jax.sharding import PartitionSpec as P

DH = 128
BLOCK = 128
MASKED_SCORE = -1e30
EPSILON = 1e-05
LOG2_E = 1.4426950408889634
MESH = pl.DeviceIdType.MESH


def rows_of(block):
    return pl.ds(pl.multiple_of(block * BLOCK, BLOCK), BLOCK)


def attention_kernel(
    sizes,
    masks,
    q_hbm,
    k_hbm,
    v_hbm,
    out,
    q_own,
    k_all,
    v_all,
    ready,
    load_sem,
    kv_send,
    kv_recv,
    att_send,
    att_recv,
    own_sem,
):
    ctx_bits, nh, groups, per_group, blocks, per_owner = sizes
    local_bits = blocks.bit_length() - 1
    width = groups * per_group * DH
    others = (nh - 1) * per_owner
    c = lax.axis_index("ctx")
    h = lax.axis_index("head")
    bit_of = [(c // 2**b) % 2 for b in range(ctx_bits)]

    loads = [
        pltpu.make_async_copy(k_hbm, k_all.at[0], load_sem.at[0]),
        pltpu.make_async_copy(v_hbm, v_all.at[0], load_sem.at[1]),
        pltpu.make_async_copy(q_hbm, q_own, load_sem.at[2]),
    ]
    for load in loads:
        load.start()

    barrier = pltpu.get_barrier_semaphore()
    for b in range(ctx_bits):
        partner = c + 2**b - 2 * 2**b * bit_of[b]
        pl.semaphore_signal(barrier, inc=1, device_id=(partner, h), device_id_type=MESH)
    for d in range(1, nh):
        pl.semaphore_signal(barrier, inc=1, device_id=(c, (h + d) % nh), device_id_type=MESH)
    pl.semaphore_wait(barrier, ctx_bits + nh - 1)

    def block_at(step):
        owner = (h + 1 + step // per_owner) % nh
        return owner, step % per_owner, owner * per_owner + step % per_owner

    def kv_copies(b, block, target):
        return [
            pltpu.make_async_remote_copy(
                src_ref=source.at[rows_of(block)],
                dst_ref=landing.at[1 + b, rows_of(block)],
                send_sem=kv_send.at[n, b, block],
                recv_sem=kv_recv.at[n, b, block],
                device_id=(target, h),
                device_id_type=MESH,
            )
            for n, (source, landing) in enumerate(((k_hbm, k_all), (v_hbm, v_all)))
        ]

    def send_step(step, carry):
        _, _, block = block_at(step)
        for b in reversed(range(ctx_bits)):

            @pl.when(bit_of[b] == 0)
            def _():
                for copy in kv_copies(b, block, c + 2**b):
                    copy.start()

        return carry

    lax.fori_loop(0, blocks, send_step, 0)
    for load in loads:
        load.wait()

    causal = lax.broadcasted_iota(jnp.int32, (BLOCK, BLOCK), 0) >= lax.broadcasted_iota(
        jnp.int32, (BLOCK, BLOCK), 1
    )

    def attend(block, step):
        for b in range(ctx_bits):

            @pl.when(bit_of[b] == 1)
            def _():
                for copy in kv_copies(b, block, c - 2**b):
                    copy.wait_recv()

        here = [(block // 2**b) % 2 for b in range(local_bits)]
        places = [(0, block)]
        places += [(0, block - here[b] * 2**b) for b in range(local_bits)]
        places += [(bit_of[b] * (1 + b), block) for b in range(ctx_bits)]
        usable = here + bit_of
        for g in range(groups):
            columns = pl.ds(g * DH, DH)
            keys = jnp.concatenate([k_all[s, rows_of(j), columns] for s, j in places], axis=0)
            values = jnp.concatenate([v_all[s, rows_of(j), columns] for s, j in places], axis=0)
            queries = jnp.concatenate(
                [
                    q_own[rows_of(block), pl.ds((g * per_group + j) * DH, DH)]
                    for j in range(per_group)
                ],
                axis=0,
            )
            scores = lax.dot_general(
                queries, keys, (((1,), (1,)), ((), ())), preferred_element_type=jnp.float32
            )
            weights, sums = [], []
            for j in range(per_group):
                bits = masks[g * per_group + j, block]
                part = scores[j * BLOCK : (j + 1) * BLOCK]
                pieces = [jnp.where(causal, part[:, :BLOCK], MASKED_SCORE)]
                for n, flag in enumerate(usable):
                    allowed = ((bits >> n) & 1) * flag
                    bias = (1 - allowed).astype(jnp.float32) * MASKED_SCORE
                    pieces.append(part[:, (n + 1) * BLOCK : (n + 2) * BLOCK] + bias)
                top = functools.reduce(jnp.maximum, pieces)
                top = jnp.max(top, axis=-1, keepdims=True)
                raised = [jnp.exp2((piece - top) * (DH**-0.5 * LOG2_E)) for piece in pieces]
                sums.append(jnp.sum(functools.reduce(jnp.add, raised), axis=-1, keepdims=True))
                weights.append(
                    jnp.concatenate([piece.astype(jnp.bfloat16) for piece in raised], axis=1)
                )
            weighted = jnp.dot(
                jnp.concatenate(weights, axis=0), values, preferred_element_type=jnp.float32
            )
            for j in range(per_group):
                ready[step, :, pl.ds((g * per_group + j) * DH, DH)] = (
                    weighted[j * BLOCK : (j + 1) * BLOCK] / sums[j]
                ).astype(jnp.bfloat16)

    def att_copy(step, owner, source_head, place):
        return pltpu.make_async_remote_copy(
            src_ref=ready.at[step],
            dst_ref=out.at[rows_of(place), pl.ds(pl.multiple_of(source_head * width, width), width)],
            send_sem=att_send.at[step],
            recv_sem=att_recv.at[source_head, place],
            device_id=(c, owner),
            device_id_type=MESH,
        )

    def own_copy(step):
        return pltpu.make_async_copy(
            ready.at[step],
            out.at[rows_of(step - others), pl.ds(pl.multiple_of(h * width, width), width)],
            own_sem.at[step - others],
        )

    def compute_step(step, carry):
        owner, place, block = block_at(step)
        attend(block, step)

        @pl.when(step < others)
        def _():
            att_copy(step, owner, h, place).start()

        @pl.when(step >= others)
        def _():
            own_copy(step).start()

        return carry

    lax.fori_loop(0, blocks, compute_step, 0)

    for place in range(per_owner):
        own_copy(others + place).wait()
        for d in range(1, nh):
            source_head = (h + d) % nh
            att_copy(0, source_head, source_head, place).wait_recv()

    def drain(step, carry):
        owner, place, block = block_at(step)
        for b in range(ctx_bits):

            @pl.when(bit_of[b] == 0)
            def _():
                for copy in kv_copies(b, block, c + 2**b):
                    copy.wait_send()

        @pl.when(step < others)
        def _():
            att_copy(step, owner, h, place).wait_send()

        return carry

    lax.fori_loop(0, blocks, drain, 0)


def norm_kernel(residual, attended, gain, stream, normed):
    summed = residual[...].astype(jnp.float32) + attended[...].astype(jnp.float32)
    stream[...] = summed.astype(jnp.bfloat16)
    mean = jnp.mean(summed * summed, axis=-1, keepdims=True)
    normed[...] = (
        summed * lax.rsqrt(mean + EPSILON) * gain[...].astype(jnp.float32)
    ).astype(jnp.bfloat16)


def shards(queries, keys, values, block_masks, residual, norm_gain):
    tokens, width = queries.shape
    kv_width = keys.shape[1]
    blocks = tokens // BLOCK
    groups = kv_width // DH
    per_group = width // kv_width
    nh = lax.axis_size("head")
    ctx_bits = lax.axis_size("ctx").bit_length() - 1
    rows, full = residual.shape
    per_owner = rows // BLOCK
    sizes = (ctx_bits, nh, groups, per_group, blocks, per_owner)
    in_any = pl.BlockSpec(memory_space=pl.ANY)
    attended = pl.pallas_call(
        functools.partial(attention_kernel, sizes),
        out_shape=jax.ShapeDtypeStruct((rows, full), jnp.bfloat16),
        in_specs=[pl.BlockSpec(memory_space=pltpu.SMEM), in_any, in_any, in_any],
        out_specs=in_any,
        scratch_shapes=[
            pltpu.VMEM((tokens, width), jnp.bfloat16),
            pltpu.VMEM((1 + ctx_bits, tokens, kv_width), jnp.bfloat16),
            pltpu.VMEM((1 + ctx_bits, tokens, kv_width), jnp.bfloat16),
            pltpu.VMEM((blocks, BLOCK, width), jnp.bfloat16),
            pltpu.SemaphoreType.DMA((3,)),
            pltpu.SemaphoreType.DMA((2, ctx_bits, blocks)),
            pltpu.SemaphoreType.DMA((2, ctx_bits, blocks)),
            pltpu.SemaphoreType.DMA((blocks,)),
            pltpu.SemaphoreType.DMA((nh, per_owner)),
            pltpu.SemaphoreType.DMA((per_owner,)),
        ],
        compiler_params=pltpu.CompilerParams(
            collective_id=0, has_side_effects=True, vmem_limit_bytes=48 * 2**20
        ),
        name="attention",
    )(block_masks, queries, keys, values)
    tile = min(rows, 64)
    by_rows = pl.BlockSpec((tile, full), lambda n: (n, 0))
    return pl.pallas_call(
        norm_kernel,
        grid=(rows // tile,),
        out_shape=(jax.ShapeDtypeStruct((rows, full), jnp.bfloat16),) * 2,
        in_specs=[by_rows, by_rows, pl.BlockSpec((1, full), lambda n: (0, 0))],
        out_specs=(by_rows, by_rows),
        compiler_params=pltpu.CompilerParams(vmem_limit_bytes=32 * 2**20),
        name="add_norm",
    )(residual, attended, norm_gain.reshape(1, full))


def solution(mesh):
    in_specs = (
        P("ctx", "head"),
        P("ctx", "head"),
        P("ctx", "head"),
        P("head", "ctx"),
        P(("ctx", "head"), None),
        P(),
    )
    out_specs = (P(("ctx", "head"), None), P(("ctx", "head"), None))
    return jax.shard_map(shards, mesh=mesh, in_specs=in_specs, out_specs=out_specs, check_vma=False)
```

time: 200 us -> 61.3 us (0.31)
  local copies, waits for them, and re-layouts: 74.3 us -> 5.07 us
  Pallas kernels: 0 us -> 55.1 us
  waiting for transfers between devices: 39.7 us -> 0 us
  matrix products: 39.4 us -> 0 us
  other arithmetic: 31 us -> 0 us
  starting transfers between devices: 12.2 us -> 0 us
    pallas_call x0 -> x2, Pallas kernels: none -> 55.1 us  [the longest x1 52.2 us: shards(): pl.pallas_call(functools.partial(attention_kernel, sizes), out_shape=jax....]
    dot_general x14 -> x0, matrix products: 39.4 us -> none  [the longest x7 28.3 us: update(): jnp.einsum('gjnqk,gnkd->gjnqd', weights.astype(jnp.bfloat16), value_part,...]
    reshape x18 -> x1, local copies, waits for them, and re-layouts: 24.8 us -> 0.71 us  [shards(): norm_gain.reshape(1, full)]
    all_to_all x1 -> x0, waiting for transfers between devices: 22.4 us -> none  [shards(): lax.all_to_all(attended, 'head', split_axis=0, concat_axis=1, tiled=True)]
    ppermute x6 -> x0, waiting for transfers between devices: 17.3 us -> none  [passed_along(): return lax.ppermute(block, axis, route)]
    unnamed x42 -> x10, local copies, waits for them, and re-layouts: 19.7 us -> 4.36 us
    reduce_sum x8 -> x0, other arithmetic: 13.9 us -> none  [the longest x7 11 us: update(): new_sum = row_sum * factor + weights.sum(-1)]
    ppermute x6 -> x0, starting transfers between devices: 7.75 us -> none  [passed_along(): return lax.ppermute(block, axis, route)]
  transfers between devices with their start and end apart: 7 -> 0, of which waited for: 2 -> 0; matrix products, arithmetic and copies ran while one was open for 35% -> 0% of each run, Pallas kernels for 0% -> 0%
where the time goes in v1:
time: 61.3 us; the launch traced here: 60.8 us
  Pallas kernels  55.1 us (90%)
  local copies, waits for them, and re-layouts  5.07 us (8%)
  between operations  0.66 us (1%)
    pallas_call x1, Pallas kernels, shards(): pl.pallas_call(functools.partial(attention_kernel, sizes), out_shape=jax....  52.2 us
    unnamed x10, local copies, waits for them, and re-layouts  4.36 us
    pallas_call x1, Pallas kernels, shards(): pl.pallas_call(norm_kernel, grid=(rows // tile,), out_shape=(jax.ShapeDty...  2.85 us

profile of v1, /device:TPU:28, one launch (start us, length us, event | category | flops | bytes accessed | tf_op | source)
XLA Modules:
  0.0 60.8 jit_solution(2412697174255227274)
XLA Ops:
  0.6 0.7 %reshape.7.gain = bf16[1,4096]{1,0:T(2,128)(2,1)S(1)} reshape(bf16[4096]{0:T(1024)(128)(2,1)} %param.11) | data formatting | bytes 16384 | tf_op jit(solution)/shard_map/reshape | solution.py:261
  1.3 0.0 copy-start
  1.4 1.6 %copy-done = bf16[1024,1024]{1,0:T(8,128)(2,1)S(1)} copy-done((bf16[1024,1024]{1,0:T(8,128)(2,1)S(1)}, bf16[1024,1024]{1,0:T(8,128)(2,1)}, u32[]{:S(2)}) %copy-start) | copy-done | bytes 2097176
  2.9 0.0 copy-start.2
  2.9 1.0 %copy-done.2 = bf16[1024,256]{1,0:T(8,128)(2,1)S(1)} copy-done((bf16[1024,256]{1,0:T(8,128)(2,1)S(1)}, bf16[1024,256]{1,0:T(8,128)(2,1)}, u32[]{:S(2)}) %copy-start.2) | copy-done | bytes 524312
  4.0 0.0 copy-start.3
  4.0 1.0 %copy-done.3 = bf16[1024,256]{1,0:T(8,128)(2,1)S(1)} copy-done((bf16[1024,256]{1,0:T(8,128)(2,1)S(1)}, bf16[1024,256]{1,0:T(8,128)(2,1)}, u32[]{:S(2)}) %copy-start.3) | copy-done | bytes 524312
  5.0 0.0 copy-start.4
  5.0 0.7 %copy-done.4 = s32[8,8]{1,0:T(8,128)S(1)} copy-done((s32[8,8]{1,0:T(8,128)S(1)}, s32[8,8]{1,0:T(8,128)}, u32[]{:S(2)}) %copy-start.4) | copy-done | bytes 280
  5.7 0.0 copy-start.1
  5.7 52.2 %attention.1.attended = bf16[256,4096]{1,0:T(8,128)(2,1)S(1)} custom-call(s32[8,8]{1,0:T(8,128)S(1)} %copy-done.4, bf16[1024,1024]{1,0:T(8,128)(2,1)S(1)} %copy-done, bf16[1024,256]{1,0:T(8,128)(2,1)S(1)} %copy-done.2, bf16[1024,256]{1,0:T(8,128)(2,1)S(1)} %copy-done.3), custom_call_target="tpu_custom_call" | custom-call | tf_op jit(solution)/shard_map/attention/pallas_call | solution.py:229
  57.9 0.0 copy-done.1
  57.9 2.8 %add_norm.1 = (bf16[256,4096]{1,0:T(8,128)(2,1)}, bf16[256,4096]{1,0:T(8,128)(2,1)}) custom-call(bf16[256,4096]{1,0:T(8,128)(2,1)S(1)} %copy-done.1, bf16[256,4096]{1,0:T(8,128)(2,1)S(1)} %attention.1.attended, bf16[1,4096]{1,0:T(2,128)(2,1)S(1)} %reshape.7.gain), custom_call_target="tpu_custom_call" | custom-call | tf_op jit(solution)/shard_map/add_norm/pallas_call | solution.py:253
Async XLA Ops:
  1.3 1.6 %copy-start = (bf16[1024,1024]{1,0:T(8,128)(2,1)S(1)}, bf16[1024,1024]{1,0:T(8,128)(2,1)}, u32[]{:S(2)}) copy-start(bf16[1024,1024]{1,0:T(8,128)(2,1)} %q_hbm.1) | copy-start | bytes 6291460
  2.9 1.0 %copy-start.2 = (bf16[1024,256]{1,0:T(8,128)(2,1)S(1)}, bf16[1024,256]{1,0:T(8,128)(2,1)}, u32[]{:S(2)}) copy-start(bf16[1024,256]{1,0:T(8,128)(2,1)} %k_hbm.1) | copy-start | bytes 1572868
  4.0 1.0 %copy-start.3 = (bf16[1024,256]{1,0:T(8,128)(2,1)S(1)}, bf16[1024,256]{1,0:T(8,128)(2,1)}, u32[]{:S(2)}) copy-start(bf16[1024,256]{1,0:T(8,128)(2,1)} %v_hbm.1) | copy-start | bytes 1572868
  5.0 0.7 %copy-start.4 = (s32[8,8]{1,0:T(8,128)S(1)}, s32[8,8]{1,0:T(8,128)}, u32[]{:S(2)}) copy-start(s32[8,8]{1,0:T(8,128)} %masks.1) | copy-start | bytes 772
  5.7 52.2 %copy-start.1 = (bf16[256,4096]{1,0:T(8,128)(2,1)S(1)}, bf16[256,4096]{1,0:T(8,128)(2,1)}, u32[]{:S(2)}) copy-start(bf16[256,4096]{1,0:T(8,128)(2,1)} %residual.1) | copy-start | bytes 6291460

commit v2 on v1

--- a/solution.py
+++ b/solution.py
@@ -21,11 +21,12 @@
 
 def attention_kernel(
     sizes,
-    masks,
+    masks_hbm,
     q_hbm,
     k_hbm,
     v_hbm,
     out,
+    masks,
     q_own,
     k_all,
     v_all,
@@ -49,6 +50,7 @@
         pltpu.make_async_copy(k_hbm, k_all.at[0], load_sem.at[0]),
         pltpu.make_async_copy(v_hbm, v_all.at[0], load_sem.at[1]),
         pltpu.make_async_copy(q_hbm, q_own, load_sem.at[2]),
+        pltpu.make_async_copy(masks_hbm, masks, load_sem.at[3]),
     ]
     for load in loads:
         load.start()
@@ -210,7 +212,7 @@
     stream[...] = summed.astype(jnp.bfloat16)
     mean = jnp.mean(summed * summed, axis=-1, keepdims=True)
     normed[...] = (
-        summed * lax.rsqrt(mean + EPSILON) * gain[...].astype(jnp.float32)
+        summed * lax.rsqrt(mean + EPSILON) * gain[...].astype(jnp.float32)[None, :]
     ).astype(jnp.bfloat16)
 
 
@@ -225,18 +227,19 @@
     rows, full = residual.shape
     per_owner = rows // BLOCK
     sizes = (ctx_bits, nh, groups, per_group, blocks, per_owner)
-    in_any = pl.BlockSpec(memory_space=pl.ANY)
+    in_hbm = pl.BlockSpec(memory_space=pltpu.HBM)
     attended = pl.pallas_call(
         functools.partial(attention_kernel, sizes),
         out_shape=jax.ShapeDtypeStruct((rows, full), jnp.bfloat16),
-        in_specs=[pl.BlockSpec(memory_space=pltpu.SMEM), in_any, in_any, in_any],
-        out_specs=in_any,
+        in_specs=[in_hbm] * 4,
+        out_specs=in_hbm,
         scratch_shapes=[
+            pltpu.SMEM(block_masks.shape, jnp.int32),
             pltpu.VMEM((tokens, width), jnp.bfloat16),
             pltpu.VMEM((1 + ctx_bits, tokens, kv_width), jnp.bfloat16),
             pltpu.VMEM((1 + ctx_bits, tokens, kv_width), jnp.bfloat16),
             pltpu.VMEM((blocks, BLOCK, width), jnp.bfloat16),
-            pltpu.SemaphoreType.DMA((3,)),
+            pltpu.SemaphoreType.DMA((4,)),
             pltpu.SemaphoreType.DMA((2, ctx_bits, blocks)),
             pltpu.SemaphoreType.DMA((2, ctx_bits, blocks)),
             pltpu.SemaphoreType.DMA((blocks,)),
@@ -247,18 +250,18 @@
             collective_id=0, has_side_effects=True, vmem_limit_bytes=48 * 2**20
         ),
         name="attention",
-    )(block_masks, queries, keys, values)
+    )(*(pltpu.with_memory_space_constraint(x, pltpu.HBM) for x in (block_masks, queries, keys, values)))
     tile = min(rows, 64)
     by_rows = pl.BlockSpec((tile, full), lambda n: (n, 0))
     return pl.pallas_call(
         norm_kernel,
         grid=(rows // tile,),
         out_shape=(jax.ShapeDtypeStruct((rows, full), jnp.bfloat16),) * 2,
-        in_specs=[by_rows, by_rows, pl.BlockSpec((1, full), lambda n: (0, 0))],
+        in_specs=[by_rows, by_rows, pl.BlockSpec((full,), lambda n: (0,))],
         out_specs=(by_rows, by_rows),
         compiler_params=pltpu.CompilerParams(vmem_limit_bytes=32 * 2**20),
         name="add_norm",
-    )(residual, attended, norm_gain.reshape(1, full))
+    )(residual, attended, norm_gain)
 
 
 def solution(mesh):

time: 61.3 us -> 55.5 us (0.905)
  local copies, waits for them, and re-layouts: 5.07 us -> 0.01 us
    unnamed x10 -> x4, local copies, waits for them, and re-layouts: 4.36 us -> 0.01 us
    reshape x1 -> x0, local copies, waits for them, and re-layouts: 0.71 us -> none  [shards(): norm_gain.reshape(1, full)]
where the time goes in v2:
time: 55.5 us; the launch traced here: 55.1 us
  Pallas kernels  54.5 us (98%)
  between operations  0.67 us (1%)
    pallas_call x1, Pallas kernels, shards(): pl.pallas_call(functools.partial(attention_kernel, sizes), out_shape=jax....  51.6 us
    pallas_call x1, Pallas kernels, shards(): pl.pallas_call(norm_kernel, grid=(rows // tile,), out_shape=(jax.ShapeDty...  2.86 us

profile of v2, /device:TPU:28, one launch (start us, length us, event | category | flops | bytes accessed | tf_op | source)
XLA Modules:
  0.0 55.1 jit_solution(6913576781931938276)
XLA Ops:
  0.6 0.0 copy-start.1
  0.6 0.0 copy-start
  0.7 51.6 %attention.1.attended = bf16[256,4096]{1,0:T(8,128)(2,1)S(1)} custom-call(s32[8,8]{1,0:T(8,128)} %masks_hbm.1, bf16[1024,1024]{1,0:T(8,128)(2,1)} %q_hbm.1, bf16[1024,256]{1,0:T(8,128)(2,1)} %k_hbm.1, bf16[1024,256]{1,0:T(8,128)(2,1)} %v_hbm.1), custom_call_target="tpu_custom_call" | custom-call | tf_op jit(solution)/shard_map/attention/pallas_call | solution.py:231
  52.3 0.0 copy-done.1
  52.3 0.0 copy-done
  52.3 2.9 %add_norm.1 = (bf16[256,4096]{1,0:T(8,128)(2,1)}, bf16[256,4096]{1,0:T(8,128)(2,1)}) custom-call(bf16[256,4096]{1,0:T(8,128)(2,1)S(1)} %copy-done, bf16[256,4096]{1,0:T(8,128)(2,1)S(1)} %attention.1.attended, bf16[4096]{0:T(1024)(128)(2,1)S(1)} %copy-done.1), custom_call_target="tpu_custom_call" | custom-call | tf_op jit(solution)/shard_map/add_norm/pallas_call | solution.py:256
Async XLA Ops:
  0.6 51.6 %copy-start.1 = (bf16[4096]{0:T(1024)(128)(2,1)S(1)}, bf16[4096]{0:T(1024)(128)(2,1)}, u32[]{:S(2)}) copy-start(bf16[4096]{0:T(1024)(128)(2,1)} %gain.1) | copy-start | bytes 24580
  0.6 51.6 %copy-start = (bf16[256,4096]{1,0:T(8,128)(2,1)S(1)}, bf16[256,4096]{1,0:T(8,128)(2,1)}, u32[]{:S(2)}) copy-start(bf16[256,4096]{1,0:T(8,128)(2,1)} %residual.1) | copy-start | bytes 6291460

commit v3 on v2

--- a/solution.py
+++ b/solution.py
@@ -99,7 +99,62 @@
         jnp.int32, (BLOCK, BLOCK), 1
     )
 
+    def sources(places, column):
+        columns = pl.ds(column * DH, DH)
+        return tuple(
+            jnp.concatenate([held[s, rows_of(j), columns] for s, j in places], axis=0)
+            for held in (k_all, v_all)
+        )
+
+    def scored(g, block, keys):
+        queries = jnp.concatenate(
+            [q_own[rows_of(block), pl.ds((g * per_group + j) * DH, DH)] for j in range(per_group)],
+            axis=0,
+        )
+        return lax.dot_general(
+            queries, keys, (((1,), (1,)), ((), ())), preferred_element_type=jnp.float32
+        )
+
+    def biased(piece, bits, level, flag):
+        allowed = ((bits >> level) & 1) * flag
+        return piece + (1 - allowed).astype(jnp.float32) * MASKED_SCORE
+
+    def raised(pieces, top):
+        weights = [jnp.exp2((piece - top) * (DH**-0.5 * LOG2_E)) for piece in pieces]
+        total = jnp.sum(functools.reduce(jnp.add, weights), axis=-1, keepdims=True)
+        return jnp.concatenate([w.astype(jnp.bfloat16) for w in weights], axis=1), total
+
+    def row_top(pieces):
+        return jnp.max(functools.reduce(jnp.maximum, pieces), axis=-1, keepdims=True)
+
+    def cut(scores, j, count):
+        part = scores[j * BLOCK : (j + 1) * BLOCK]
+        return [part[:, n * BLOCK : (n + 1) * BLOCK] for n in range(count)]
+
     def attend(block, step):
+        here = [(block // 2**b) % 2 for b in range(local_bits)]
+        near = [(0, block)] + [(0, block - here[b] * 2**b) for b in range(local_bits)]
+        far = [(bit_of[b] * (1 + b), block) for b in range(ctx_bits)]
+        partial = []
+        for g in range(groups):
+            keys, values = sources(near, g)
+            scores = scored(g, block, keys)
+            weights, tops, sums = [], [], []
+            for j in range(per_group):
+                bits = masks[g * per_group + j, block]
+                pieces = cut(scores, j, 1 + local_bits)
+                pieces = [jnp.where(causal, pieces[0], MASKED_SCORE)] + [
+                    biased(piece, bits, b, here[b]) for b, piece in enumerate(pieces[1:])
+                ]
+                tops.append(row_top(pieces))
+                weight, total = raised(pieces, tops[-1])
+                weights.append(weight)
+                sums.append(total)
+            weighted = jnp.dot(
+                jnp.concatenate(weights, axis=0), values, preferred_element_type=jnp.float32
+            )
+            partial.append((tops, sums, weighted))
+
         for b in range(ctx_bits):
 
             @pl.when(bit_of[b] == 1)
@@ -107,47 +162,30 @@
                 for copy in kv_copies(b, block, c - 2**b):
                     copy.wait_recv()
 
-        here = [(block // 2**b) % 2 for b in range(local_bits)]
-        places = [(0, block)]
-        places += [(0, block - here[b] * 2**b) for b in range(local_bits)]
-        places += [(bit_of[b] * (1 + b), block) for b in range(ctx_bits)]
-        usable = here + bit_of
         for g in range(groups):
-            columns = pl.ds(g * DH, DH)
-            keys = jnp.concatenate([k_all[s, rows_of(j), columns] for s, j in places], axis=0)
-            values = jnp.concatenate([v_all[s, rows_of(j), columns] for s, j in places], axis=0)
-            queries = jnp.concatenate(
-                [
-                    q_own[rows_of(block), pl.ds((g * per_group + j) * DH, DH)]
-                    for j in range(per_group)
-                ],
-                axis=0,
-            )
-            scores = lax.dot_general(
-                queries, keys, (((1,), (1,)), ((), ())), preferred_element_type=jnp.float32
-            )
-            weights, sums = [], []
+            tops, sums, weighted = partial[g]
+            keys, values = sources(far, g)
+            scores = scored(g, block, keys)
+            weights, factors, totals = [], [], []
             for j in range(per_group):
                 bits = masks[g * per_group + j, block]
-                part = scores[j * BLOCK : (j + 1) * BLOCK]
-                pieces = [jnp.where(causal, part[:, :BLOCK], MASKED_SCORE)]
-                for n, flag in enumerate(usable):
-                    allowed = ((bits >> n) & 1) * flag
-                    bias = (1 - allowed).astype(jnp.float32) * MASKED_SCORE
-                    pieces.append(part[:, (n + 1) * BLOCK : (n + 2) * BLOCK] + bias)
-                top = functools.reduce(jnp.maximum, pieces)
-                top = jnp.max(top, axis=-1, keepdims=True)
-                raised = [jnp.exp2((piece - top) * (DH**-0.5 * LOG2_E)) for piece in pieces]
-                sums.append(jnp.sum(functools.reduce(jnp.add, raised), axis=-1, keepdims=True))
-                weights.append(
-                    jnp.concatenate([piece.astype(jnp.bfloat16) for piece in raised], axis=1)
-                )
-            weighted = jnp.dot(
+                pieces = [
+                    biased(piece, bits, local_bits + b, bit_of[b])
+                    for b, piece in enumerate(cut(scores, j, ctx_bits))
+                ]
+                top = jnp.maximum(tops[j], row_top(pieces))
+                weight, total = raised(pieces, top)
+                factor = jnp.exp2((tops[j] - top) * (DH**-0.5 * LOG2_E))
+                weights.append(weight)
+                factors.append(factor)
+                totals.append(sums[j] * factor + total)
+            added = jnp.dot(
                 jnp.concatenate(weights, axis=0), values, preferred_element_type=jnp.float32
             )
             for j in range(per_group):
+                lines = slice(j * BLOCK, (j + 1) * BLOCK)
                 ready[step, :, pl.ds((g * per_group + j) * DH, DH)] = (
-                    weighted[j * BLOCK : (j + 1) * BLOCK] / sums[j]
+                    (weighted[lines] * factors[j] + added[lines]) / totals[j]
                 ).astype(jnp.bfloat16)
 
     def att_copy(step, owner, source_head, place):
@@ -251,7 +289,7 @@
         ),
         name="attention",
     )(*(pltpu.with_memory_space_constraint(x, pltpu.HBM) for x in (block_masks, queries, keys, values)))
-    tile = min(rows, 64)
+    tile = min(rows, 128)
     by_rows = pl.BlockSpec((tile, full), lambda n: (n, 0))
     return pl.pallas_call(
         norm_kernel,

time: 55.5 us -> 54.5 us (0.982)
  Pallas kernels: 54.5 us -> 53.4 us
    pallas_call x1, Pallas kernels: 51.6 us -> 50.8 us  [shards(): pl.pallas_call(functools.partial(attention_kernel, sizes), out_shape=jax....]
where the time goes in v3:
time: 54.5 us; the launch traced here: 54.1 us
  Pallas kernels  53.4 us (98%)
  between operations  0.67 us (1%)
    pallas_call x1, Pallas kernels, shards(): pl.pallas_call(functools.partial(attention_kernel, sizes), out_shape=jax....  50.8 us
    pallas_call x1, Pallas kernels, shards(): pl.pallas_call(norm_kernel, grid=(rows // tile,), out_shape=(jax.ShapeDty...  2.65 us

profile of v3, /device:TPU:28, one launch (start us, length us, event | category | flops | bytes accessed | tf_op | source)
XLA Modules:
  0.0 54.1 jit_solution(11527448140590672271)
XLA Ops:
  0.6 0.0 copy-start.1
  0.6 0.0 copy-start
  0.7 50.8 %attention.1.attended = bf16[256,4096]{1,0:T(8,128)(2,1)S(1)} custom-call(s32[8,8]{1,0:T(8,128)} %masks_hbm.1, bf16[1024,1024]{1,0:T(8,128)(2,1)} %q_hbm.1, bf16[1024,256]{1,0:T(8,128)(2,1)} %k_hbm.1, bf16[1024,256]{1,0:T(8,128)(2,1)} %v_hbm.1), custom_call_target="tpu_custom_call" | custom-call | tf_op jit(solution)/shard_map/attention/pallas_call | solution.py:269
  51.5 0.0 copy-done.1
  51.5 0.0 copy-done
  51.5 2.7 %add_norm.1 = (bf16[256,4096]{1,0:T(8,128)(2,1)}, bf16[256,4096]{1,0:T(8,128)(2,1)}) custom-call(bf16[256,4096]{1,0:T(8,128)(2,1)S(1)} %copy-done, bf16[256,4096]{1,0:T(8,128)(2,1)S(1)} %attention.1.attended, bf16[4096]{0:T(1024)(128)(2,1)S(1)} %copy-done.1), custom_call_target="tpu_custom_call" | custom-call | tf_op jit(solution)/shard_map/add_norm/pallas_call | solution.py:294
Async XLA Ops:
  0.6 50.8 %copy-start.1 = (bf16[4096]{0:T(1024)(128)(2,1)S(1)}, bf16[4096]{0:T(1024)(128)(2,1)}, u32[]{:S(2)}) copy-start(bf16[4096]{0:T(1024)(128)(2,1)} %gain.1) | copy-start | bytes 24580
  0.6 50.8 %copy-start = (bf16[256,4096]{1,0:T(8,128)(2,1)S(1)}, bf16[256,4096]{1,0:T(8,128)(2,1)}, u32[]{:S(2)}) copy-start(bf16[256,4096]{1,0:T(8,128)(2,1)} %residual.1) | copy-start | bytes 6291460

commit v4 on v3

--- a/solution.py
+++ b/solution.py
@@ -82,12 +82,12 @@
 
     def send_step(step, carry):
         _, _, block = block_at(step)
-        for b in reversed(range(ctx_bits)):
-
-            @pl.when(bit_of[b] == 0)
-            def _():
-                for copy in kv_copies(b, block, c + 2**b):
-                    copy.start()
+        for n in range(2):
+            for b in reversed(range(ctx_bits)):
+
+                @pl.when(bit_of[b] == 0)
+                def _():
+                    kv_copies(b, block, c + 2**b)[n].start()
 
         return carry
 
@@ -99,12 +99,9 @@
         jnp.int32, (BLOCK, BLOCK), 1
     )
 
-    def sources(places, column):
+    def gathered(held, places, column):
         columns = pl.ds(column * DH, DH)
-        return tuple(
-            jnp.concatenate([held[s, rows_of(j), columns] for s, j in places], axis=0)
-            for held in (k_all, v_all)
-        )
+        return jnp.concatenate([held[s, rows_of(j), columns] for s, j in places], axis=0)
 
     def scored(g, block, keys):
         queries = jnp.concatenate(
@@ -137,7 +134,7 @@
         far = [(bit_of[b] * (1 + b), block) for b in range(ctx_bits)]
         partial = []
         for g in range(groups):
-            keys, values = sources(near, g)
+            keys, values = gathered(k_all, near, g), gathered(v_all, near, g)
             scores = scored(g, block, keys)
             weights, tops, sums = [], [], []
             for j in range(per_group):
@@ -155,16 +152,18 @@
             )
             partial.append((tops, sums, weighted))
 
-        for b in range(ctx_bits):
-
-            @pl.when(bit_of[b] == 1)
-            def _():
-                for copy in kv_copies(b, block, c - 2**b):
-                    copy.wait_recv()
-
+        def arrived(n):
+            for b in range(ctx_bits):
+
+                @pl.when(bit_of[b] == 1)
+                def _():
+                    kv_copies(b, block, c - 2**b)[n].wait_recv()
+
+        arrived(0)
+        joined = []
         for g in range(groups):
-            tops, sums, weighted = partial[g]
-            keys, values = sources(far, g)
+            tops, sums, _ = partial[g]
+            keys = gathered(k_all, far, g)
             scores = scored(g, block, keys)
             weights, factors, totals = [], [], []
             for j in range(per_group):
@@ -179,6 +178,12 @@
                 weights.append(weight)
                 factors.append(factor)
                 totals.append(sums[j] * factor + total)
+            joined.append((weights, factors, totals))
+        arrived(1)
+        for g in range(groups):
+            weighted = partial[g][2]
+            weights, factors, totals = joined[g]
+            values = gathered(v_all, far, g)
             added = jnp.dot(
                 jnp.concatenate(weights, axis=0), values, preferred_element_type=jnp.float32
             )

time: 54.5 us -> 53.8 us (0.987)
  Pallas kernels: 53.4 us -> 52.7 us
    pallas_call x1, Pallas kernels: 50.8 us -> 50.1 us  [shards(): pl.pallas_call(functools.partial(attention_kernel, sizes), out_shape=jax....]
where the time goes in v4:
time: 53.8 us; the launch traced here: 53.4 us
  Pallas kernels  52.7 us (98%)
  between operations  0.67 us (1%)
    pallas_call x1, Pallas kernels, shards(): pl.pallas_call(functools.partial(attention_kernel, sizes), out_shape=jax....  50.1 us
    pallas_call x1, Pallas kernels, shards(): pl.pallas_call(norm_kernel, grid=(rows // tile,), out_shape=(jax.ShapeDty...  2.65 us

profile of v4, /device:TPU:28, one launch (start us, length us, event | category | flops | bytes accessed | tf_op | source)
XLA Modules:
  0.0 53.4 jit_solution(5524550506307894736)
XLA Ops:
  0.6 0.0 copy-start.1
  0.6 0.0 copy-start
  0.7 50.1 %attention.1.attended = bf16[256,4096]{1,0:T(8,128)(2,1)S(1)} custom-call(s32[8,8]{1,0:T(8,128)} %masks_hbm.1, bf16[1024,1024]{1,0:T(8,128)(2,1)} %q_hbm.1, bf16[1024,256]{1,0:T(8,128)(2,1)} %k_hbm.1, bf16[1024,256]{1,0:T(8,128)(2,1)} %v_hbm.1), custom_call_target="tpu_custom_call" | custom-call | tf_op jit(solution)/shard_map/attention/pallas_call | solution.py:274
  50.7 0.0 copy-done.1
  50.7 0.0 copy-done
  50.7 2.7 %add_norm.1 = (bf16[256,4096]{1,0:T(8,128)(2,1)}, bf16[256,4096]{1,0:T(8,128)(2,1)}) custom-call(bf16[256,4096]{1,0:T(8,128)(2,1)S(1)} %copy-done, bf16[256,4096]{1,0:T(8,128)(2,1)S(1)} %attention.1.attended, bf16[4096]{0:T(1024)(128)(2,1)S(1)} %copy-done.1), custom_call_target="tpu_custom_call" | custom-call | tf_op jit(solution)/shard_map/add_norm/pallas_call | solution.py:299
Async XLA Ops:
  0.6 50.1 %copy-start.1 = (bf16[4096]{0:T(1024)(128)(2,1)S(1)}, bf16[4096]{0:T(1024)(128)(2,1)}, u32[]{:S(2)}) copy-start(bf16[4096]{0:T(1024)(128)(2,1)} %gain.1) | copy-start | bytes 24580
  0.6 50.1 %copy-start = (bf16[256,4096]{1,0:T(8,128)(2,1)S(1)}, bf16[256,4096]{1,0:T(8,128)(2,1)}, u32[]{:S(2)}) copy-start(bf16[256,4096]{1,0:T(8,128)(2,1)} %residual.1) | copy-start | bytes 6291460
